TPU v7x, 128 devices: a whole 4x4x4 slice. The times are simulated.
128 devices in a mesh: pipe: 4 (over x), tp: 8 (over y, z_hi), dp: 4 (over z_lo, core).
Axes of the slice: x: 4, y: 4, z: 4 (z_hi: 2, z_lo: 2; z = z_hi * 2 + z_lo), core: 2. Of those that a mesh axis runs over, the one named last changes fastest.
Arguments:
- upstream: bfloat16 [4, 6656, 8192], P('pipe', ('dp', 'tp')), may hold values from -6 to 6
- saved_input: bfloat16 [4, 2, 6656, 4096], P('pipe', None, 'dp', 'tp'), may hold values from -6 to 6
- weight: bfloat16 [4, 4096, 8192], P('pipe', 'tp', 'dp'), may hold values from -0.0625 to 0.0625
- weight_noise: bfloat16 [4, 4096, 8192], P('pipe', 'tp', 'dp'), may hold values from -0.03125 to 0.03125
- levels: int32 [4, 32, 64], P('pipe', 'tp', 'dp'), may hold values from 1 to 4
- plan: int32 [4], replicated, may hold values from 0 to 1
Outputs:
- master_grad: float32 [4, 4096, 8192], P('pipe', 'tp', 'dp')
- passed: bfloat16 [4, 6656, 4096], P('pipe', ('dp', 'tp'))
All inputs are finite; a program needn't handle non-finite values.
Results may differ from a plain program's by a relative error of at most 0.015.
Values may be sent and summed in bfloat16 or wider, within the bound.
A program may use at most 192 MiB of HBM per device.

v0:
```python
import jax
import jax.numpy as jnp
from jax import lax
from jax.sharding import PartitionSpec as P

clip_step = 0.006


def shifted(block, axis, distance):
    devices = range(lax.axis_size(axis))
    route = [(i - distance, i) for i in devices if i - distance in devices]
    return lax.ppermute(block, axis, route)


def local(upstream, saved_input, weight, weight_noise, levels, plan):
    section = lax.axis_index("pipe")
    picked = plan[section]
    chosen = lax.dynamic_index_in_dim(saved_input[0], picked, 0, keepdims=False)
    grad_in = upstream[0]
    tok_dev = grad_in.shape[0]
    tp_count = lax.axis_size("tp")
    dp_count = lax.axis_size("dp")
    noisy = weight[0].astype(jnp.float32) + weight_noise[0].astype(jnp.float32)
    in_rows, out_cols = noisy.shape
    tile_rows = levels.shape[1]
    tile_cols = levels.shape[2]
    tile_size = in_rows // tile_rows
    bounds = (levels[0].astype(jnp.float32) * clip_step)[:, None, :, None]
    noisy_tiles = noisy.reshape(tile_rows, tile_size, tile_cols, tile_size)
    effective = (
        jnp.clip(noisy_tiles, -bounds, bounds).reshape(in_rows, out_cols).astype(jnp.bfloat16)
    )
    inside = (jnp.abs(noisy_tiles) <= bounds).reshape(in_rows, out_cols).astype(jnp.float32)
    norm_factor = 1.0 / jnp.sqrt(jnp.float32(tok_dev * tp_count * dp_count))
    grad_full = lax.all_gather(grad_in, "tp", axis=0, tiled=True)
    columns = grad_full
    branch = lax.dot_general(
        columns,
        lax.all_gather(effective, "dp", axis=1, tiled=True),
        (((1,), (1,)), ((), ())),
        preferred_element_type=jnp.float32,
    )
    columns = grad_full
    owned = lax.psum_scatter(
        lax.dot_general(
            columns, chosen, (((0,), (0,)), ((), ())), preferred_element_type=jnp.float32
        ).astype(jnp.bfloat16),
        "dp",
        scatter_dimension=0,
        tiled=True,
    ).astype(jnp.float32)
    grad_owned = owned.T
    master = grad_owned * inside * norm_factor
    branch_out = branch.astype(jnp.bfloat16)
    moved = lax.all_to_all(branch_out, "tp", split_axis=0, concat_axis=1, tiled=True)
    passed = shifted(moved, "pipe", -1)
    return (master[None], passed[None])


def solution(mesh):
    placed = (
        P("pipe", ("dp", "tp"), None),
        P("pipe", None, "dp", "tp"),
        P("pipe", "tp", "dp"),
        P("pipe", "tp", "dp"),
        P("pipe", "tp", "dp"),
        P(),
    )
    return jax.shard_map(
        local,
        mesh=mesh,
        in_specs=placed,
        out_specs=(P("pipe", "tp", "dp"), P("pipe", ("dp", "tp"), None)),
        check_vma=False,
    )
```

profile of v0, /device:TPU:6, one launch (start us, length us, event | category | flops | bytes accessed | tf_op | source)
XLA Modules:
  0.0 495.5 jit_solution(3897639897268168351)
XLA Ops:
  7.2 0.0 all-gather.6.cloned.1.call-start
  7.2 0.7 all-gather.6.cloned.1.call-update
  7.9 0.0 all-gather.4.cloned.1.call-start
  8.0 0.9 fusion.23
  8.9 1.3 multiply_bitcast_fusion
  10.2 0.3 le.11
  10.5 0.3 max.15
  10.9 1.7 copy-done.2
  12.6 3.7 fusion.11
  16.3 0.0 all-gather.4.cloned.1.call-update
  16.3 0.2 reduce-scatter.2.cloned.1.call-start
  16.6 0.6 dynamic_slice.7
  19.1 275.9 %all-gather.6.cloned.1.call-done = bf16[1,1664,8192]{2,1,0:T(8,128)(2,1)} async-done(((bf16[1,208,8192]{2,1,0:T(8,128)(2,1)}), bf16[1,1664,8192]{2,1,0:T(8,128)(2,1)}) %all-gather.6.cloned.1.call-update) | async-done | bytes 27262992 | tf_op jit(solution)/shard_map/all_gather | solution.py:35
  295.0 22.6 %fusion.7 = bf16[8192,512]{0,1:T(8,128)(2,1)} fusion(bf16[1,1664,8192]{2,1,0:T(8,128)(2,1)} %all-gather.6.cloned.1.call-done, bf16[1,2,1664,512]{3,2,1,0:T(8,128)(2,1)S(1)} %copy-done, s32[]{:T(128)S(6)} %select_n.8), kind=kOutput, calls=%fused_computation.5 | convolution fusion | flops 13962838016 | bytes 37355524 | tf_op jit(solution)/shard_map/dot_general | solution.py:45
  317.7 57.5 %all-gather.4.cloned.1.call-done = bf16[512,8192]{1,0:T(8,128)(2,1)} async-done(((bf16[512,2048]{1,0:T(8,128)(2,1)}), bf16[512,8192]{1,0:T(8,128)(2,1)}) %all-gather.4.cloned.1.call-update) | async-done | bytes 8388624 | tf_op jit(solution)/shard_map/all_gather | solution.py:39
  375.2 20.9 %fusion.17 = bf16[1664,512]{0,1:T(8,128)(2,1)S(1)} fusion(bf16[512,8192]{1,0:T(8,128)(2,1)} %all-gather.4.cloned.1.call-done, bf16[1,1664,8192]{2,1,0:T(8,128)(2,1)} %all-gather.6.cloned.1.call-done), kind=kOutput, calls=%fused_computation.16 | convolution fusion | flops 13959495680 | bytes 37355520 | tf_op jit(solution)/shard_map/dot_general | solution.py:37
  396.2 1.4 copy.10
  397.6 34.6 %all_to_all.19 = bf16[8,208,512]{2,1,0:T(8,128)(2,1)S(1)} all-to-all(bf16[8,208,512]{2,1,0:T(8,128)(2,1)S(1)} %bitcast.64), channel_id=1, replica_groups=mesh['pipe'=4,'tp'=8,'dp'=4] {'tp'}, dimensions={0} | all-to-all | bytes 3407872 | tf_op jit(solution)/shard_map/all_to_all | solution.py:55
  432.2 0.2 copy.12
  432.4 4.0 collective-permute-start
  436.4 35.5 %collective-permute-done = bf16[208,4096]{1,0:T(8,128)(2,1)} collective-permute-done((bf16[208,4096]{1,0:T(8,128)(2,1)S(1)}, bf16[208,4096]{1,0:T(8,128)(2,1)}, u32[]{:S(2)}, u32[]{:S(2)}) %collective-permute-start) | collective-permute-done | bytes 1703968 | tf_op jit(solution)/shard_map/ppermute | solution.py:12
  471.9 5.3 %reduce-scatter.2.cloned.1.call-done = bf16[2048,512]{0,1:T(8,128)(2,1)} async-done(((bf16[8192,512]{0,1:T(8,128)(2,1)}), bf16[2048,512]{0,1:T(8,128)(2,1)}) %reduce-scatter.2.cloned.1.call-update) | async-done | bytes 2097168 | tf_op jit(solution)/shard_map/reduce_scatter | solution.py:44
  477.2 8.9 %fusion.13 = f32[1,512,2048]{2,1,0:T(8,128)} fusion(bf16[2048,512]{0,1:T(8,128)(2,1)} %reduce-scatter.2.cloned.1.call-done, bf16[1,512,2048]{2,1,0:T(8,128)(2,1)} %param.9, bf16[1,512,2048]{2,1,0:T(8,128)(2,1)} %param.8, f32[64,8,16,128]{3,2,1,0:T(8,128)} %bitcast.62), kind=kLoop, calls=%fused_computation.12 | loop fusion | flops 8388608 | bytes 14680064 | tf_op jit(solution)/shard_map/broadcast_in_dim | solution.py:57
  486.1 2.8 copy.19
  (12 shorter events, 0.0 us)
Async XLA Ops:
  7.2 287.9 %copy-start = (bf16[1,2,1664,512]{3,2,1,0:T(8,128)(2,1)S(1)}, bf16[1,2,1664,512]{3,2,1,0:T(8,128)(2,1)}, u32[]{:S(2)}) copy-start(bf16[1,2,1664,512]{3,2,1,0:T(8,128)(2,1)} %param.7) | copy-start | bytes 10223620
  7.2 287.9 %all-gather.6.cloned.1.call-start = ((), (), s32[]{:S(2)}) async-start(), calls=%async_computation.4 | async-start | bytes 30670848 | tf_op jit(solution)/shard_map/all_gather | solution.py:35
  7.9 367.3 %all-gather.4.cloned.1.call-start = ((), (), s32[]{:S(2)}) async-start(), calls=%async_computation.3 | async-start | bytes 10485760 | tf_op jit(solution)/shard_map/all_gather | solution.py:39
  8.0 4.6 copy-start.3
  8.0 4.6 copy-start.4
  10.5 2.1 copy-start.2
  12.6 4.0 copy-start.5
  16.3 460.9 %reduce-scatter.2.cloned.1.call-start = ((), (), s32[]{:S(2)}) async-start(), calls=%async_computation.2 | async-start | bytes 10485760 | tf_op jit(solution)/shard_map/reduce_scatter | solution.py:44
  432.4 39.5 %collective-permute-start = (bf16[208,4096]{1,0:T(8,128)(2,1)S(1)}, bf16[208,4096]{1,0:T(8,128)(2,1)}, u32[]{:S(2)}, u32[]{:S(2)}) collective-permute-start(bf16[208,4096]{1,0:T(8,128)(2,1)S(1)} %bitcast.66), channel_id=1, source_target_pairs={{32,0},{64,32},{96,64},{33,1},{65,33},{97,65},{34,2},{66,34},{98,6... | collective-permute-start | bytes 5111816 | tf_op jit(solution)/shard_map/ppermute | solution.py:12
  477.2 11.7 %copy-start.1 = (bf16[1,2,1664,512]{3,2,1,0:T(8,128)(2,1)S(1)}, bf16[1,2,1664,512]{3,2,1,0:T(8,128)(2,1)}, u32[]{:S(2)}) copy-start(bf16[1,2,1664,512]{3,2,1,0:T(8,128)(2,1)} %param.7) | copy-start | bytes 10223620
Sparse Core Ops, SparseCore 0:
  10.4 284.6 all-gather.5
  297.3 77.9 all-gather.3
  377.7 99.4 reduce-scatter.1
where the time goes:
time: 497 us; the launch traced here: 495 us
  waiting for transfers between devices  375 us (75%)
  matrix products  43.6 us (9%)
  blocking collectives  34.6 us (7%)
  between operations  15.8 us (3%)
  other arithmetic  14.8 us (3%)
  local copies, waits for them, and re-layouts  7.43 us (1%)
    all_gather x1, waiting for transfers between devices, local(): grad_full = lax.all_gather(grad_in, 'tp', axis=0, tiled=True)  276 us
    all_gather x1, waiting for transfers between devices, local(): lax.all_gather(effective, 'dp', axis=1, tiled=True)  57.5 us
    ppermute x1, waiting for transfers between devices, shifted(): return lax.ppermute(block, axis, route)  35.5 us
    all_to_all x1, blocking collectives, local(): lax.all_to_all(branch_out, 'tp', split_axis=0, concat_axis=1, tiled=True)  34.6 us
    dot_general x1, matrix products, local(): lax.dot_general(columns, chosen, (((0,), (0,)), ((), ())), preferred_elem...  22.6 us
    dot_general x1, matrix products, local(): lax.dot_general(columns, lax.all_gather(effective, 'dp', axis=1, tiled=Tr...  20.9 us
  transfers between devices with their start and end apart: 4, of which 4 were waited for; matrix products, arithmetic and copies ran while one was open for 11% of the time, Pallas kernels for 0%

commit v1 on v0

v1 whole, which is shorter than its diff:
```python
import functools

import jax
import jax.numpy as jnp
from jax import lax
from jax.experimental import pallas as pl
from jax.experimental.pallas import tpu as pltpu
from jax.sharding import PartitionSpec as P

clip_step = 0.006
MESH = pl.DeviceIdType.MESH
TILE = 128


def aligned(start, size, step=128):
    return pl.ds(pl.multiple_of(start, step), size)


def relay_kernel(
    up, picked, weight, noise, levels,
    master, passed,
    ubuf, wbuf, cbuf, ctbuf, acc, gself, gopp, gside, ghalf, gfull, bsend, brecv, bout,
    u_loc, u_sib_s, u_sib_r, u_own_s, u_own_r, u_fwd_s, u_fwd_r,
    c_loc, c_opp_s, c_opp_r, c_sib_s, c_sib_r,
    w_own_s, w_own_r, w_fwd_s, w_fwd_r,
    g_half_s, g_half_r, g_full_s, g_full_r,
    b_sib_s, b_sib_r, b_out_s, b_out_r, m_out,
):
    tok = up.shape[0]
    rows = tok * 4
    quarter = weight.shape[1]
    blk = weight.shape[0]
    half = blk // 2
    subs = 4
    cw = quarter // subs
    feats = 2 * blk

    x = lax.axis_index("pipe")
    tp = lax.axis_index("tp")
    dp = lax.axis_index("dp")
    y, zh = tp // 2, tp % 2
    zl, c = dp // 2, dp % 2
    z = 2 * zh + zl
    oc = 1 - c

    def at(xx, yy, zz, cc):
        xx, yy, zz = xx % 4, yy % 4, zz % 4
        return (xx, yy * 2 + zz // 2, (zz % 2) * 2 + cc)

    sib = at(x, y, z, oc)
    opp = at(x, y, z + 2, c)
    ynb = (at(x, y + 1, z, c), at(x, y + 3, z, c))
    znb = (at(x, y, z + 1, c), at(x, y, z + 3, c))
    zp = (zh + zl) % 2
    zside = (zp, 1 - zp)

    barrier = pltpu.get_barrier_semaphore()
    greet = [sib, opp, *ynb, *znb] + [at(x + 1, y + j, z, c) for j in range(4)]
    for one in greet:
        pl.semaphore_signal(barrier, inc=1, device_id=one, device_id_type=MESH)

    def remote(src, dst, s, r, to):
        return pltpu.make_async_remote_copy(
            src_ref=src, dst_ref=dst, send_sem=s, recv_sem=r, device_id=to, device_id_type=MESH
        )

    def urow(yy, cc):
        return aligned(cc * rows + yy * tok, tok, 16)

    def ucol(k):
        return aligned((k % 2) * quarter + (k // 2) * cw, cw)

    def hcol(k, cc):
        return aligned(((zl + k) % 2) * (2 * quarter) + cc * quarter + (k // 2) * cw, cw)

    def u_local(k):
        return pltpu.make_async_copy(up.at[:, hcol(k, c)], ubuf.at[urow(y, c), ucol(k)], u_loc.at[k])

    def u_sib(k):
        return remote(up.at[:, hcol(k, oc)], ubuf.at[urow(y, c), ucol(k)], u_sib_s.at[k], u_sib_r.at[k], sib)

    def u_own(k, d, mine):
        cc = c if mine else oc
        src = up.at[:, hcol(k, c)] if mine else ubuf.at[urow(y, oc), ucol(k)]
        at_sem = (k, d, cc)
        return remote(src, ubuf.at[urow(y, cc), ucol(k)], u_own_s.at[at_sem], u_own_r.at[at_sem], ynb[d])

    def u_own_wait(k, d, cc):
        ref = ubuf.at[urow(y, cc), ucol(k)]
        return remote(ref, ref, u_own_s.at[k, d, cc], u_own_r.at[k, d, cc], ynb[d])

    def u_fwd(k, d):
        yy = (y + 3) % 4 if d == 0 else (y + 1) % 4
        ref = ubuf.at[urow(yy, d), ucol(k)]
        return remote(ref, ref, u_fwd_s.at[k, d], u_fwd_r.at[k, d], ynb[d])

    def issue_own(k):
        for d in range(2):
            u_own(k, d, True).start()
        u_sib(k).wait_recv()
        for d in range(2):
            u_own(k, d, False).start()

    def y_stage(k):
        for d in range(2):
            u_own_wait(k, d, d).wait_recv()
            u_fwd(k, d).start()

        @pl.when(k + 2 < 2 * subs)
        def _():
            issue_own(k + 2)

    def u_ready(k):
        u_local(k).wait()
        for d in range(2):
            u_own_wait(k, d, 1 - d).wait_recv()
        for d in range(2):
            u_fwd(k, d).wait_recv()

    def wref(hi, first, count, side, p):
        return wbuf.at[aligned(hi * blk + first, count), aligned(side * quarter + p * cw, cw)]

    def w_own(p, d):
        return remote(wref(zh, 0, blk, 0, p), wref(zh, 0, blk, 1, p), w_own_s.at[p, d], w_own_r.at[p, d], znb[d])

    def w_fwd(p, d):
        hi = zside[1 - d]
        return remote(
            wref(hi, d * half, half, 1, p), wref(hi, d * half, half, 0, p), w_fwd_s.at[p, d], w_fwd_r.at[p, d], znb[d]
        )

    def clip_weights(t, _):
        i, p = t % 4, t // 4
        for j in range(cw // TILE):
            bound = levels[i, p * (cw // TILE) + j].astype(jnp.float32) * clip_step
            place = (aligned(i * TILE, TILE), aligned(p * cw + j * TILE, TILE))
            noisy = weight[place].astype(jnp.float32) + noise[place].astype(jnp.float32)
            wbuf[aligned(zh * blk + i * TILE, TILE), aligned(p * cw + j * TILE, TILE)] = jnp.minimum(
                jnp.maximum(noisy, -bound), bound
            ).astype(jnp.bfloat16)
        return 0

    def ccol(hi):
        return aligned(hi * blk, blk)

    crows = aligned(c * rows, rows, 16)
    c_local = pltpu.make_async_copy(picked.at[zh], cbuf.at[crows, ccol(zh)], c_loc.at[0])
    c_opp = remote(picked.at[1 - zh], cbuf.at[crows, ccol(zh)], c_opp_s.at[0], c_opp_r.at[0], opp)
    c_sib = remote(cbuf.at[crows], cbuf.at[crows], c_sib_s.at[0], c_sib_r.at[0], sib)

    def turn(t, _):
        place = aligned(t * TILE, TILE)
        ctbuf[:, place] = cbuf[place, :].T
        return 0

    def tile_grad(hi, k, n):
        cols = aligned((k % 2) * quarter + (k // 2) * cw + n * 256, 256)
        return jnp.dot(ctbuf[aligned(hi * blk, blk), :], ubuf[:, cols], preferred_element_type=jnp.float32)

    def g_half(s, d):
        return remote(
            gopp.at[s, pl.ds(d * half, half)], ghalf.at[d, s], g_half_s.at[s, d], g_half_r.at[s, d], znb[d]
        )

    def g_full(s, d):
        return remote(gside.at[d, s], gfull.at[d, s], g_full_s.at[s, d], g_full_r.at[s, d], znb[d])

    def grad_same(s):
        u_ready(2 * s)

        def body(n, _):
            gself[:, aligned(s * cw + n * 256, 256)] = tile_grad(zh, 2 * s, n)
            gopp[s, :, aligned(n * 256, 256)] = tile_grad(1 - zh, 2 * s, n).astype(jnp.bfloat16)
            return 0

        lax.fori_loop(0, cw // 256, body, 0)
        for d in range(2):
            g_half(s, d).start()

    def grad_side(s):
        u_ready(2 * s + 1)

        def body(n, _):
            for d in range(2):
                gside[d, s, :, aligned(n * 256, 256)] = tile_grad(zside[d], 2 * s + 1, n).astype(jnp.bfloat16)
            return 0

        lax.fori_loop(0, cw // 256, body, 0)

    def combine(s):
        for d in range(2):
            g_half(s, d).wait_recv()
            place = pl.ds(d * half, half)
            gside[d, s, place] = (
                gside[d, s, place].astype(jnp.float32) + ghalf[d, s].astype(jnp.float32)
            ).astype(jnp.bfloat16)
            g_full(s, d).start()

    def master_copy(s):
        place = aligned(s * cw, cw)
        return pltpu.make_async_copy(gself.at[:, place], master.at[:, place], m_out.at[s])

    def finish(s):
        for d in range(2):
            g_full(s, d).wait_recv()

        def body(i, _):
            line = aligned(i * TILE, TILE)
            for j in range(cw // TILE):
                bound = levels[i, s * (cw // TILE) + j].astype(jnp.float32) * clip_step
                place = (line, aligned(s * cw + j * TILE, TILE))
                noisy = weight[place].astype(jnp.float32) + noise[place].astype(jnp.float32)
                inner = pl.ds(j * TILE, TILE)
                total = gself[place] + gfull[0, s, line, inner].astype(jnp.float32)
                total = total + gfull[1, s, line, inner].astype(jnp.float32)
                gself[place] = jnp.where(jnp.abs(noisy) <= bound, total, 0.0)
            return 0

        lax.fori_loop(0, blk // TILE, body, 0)
        master_copy(s).start()

    def w_ready(p):
        for d in range(2):
            w_fwd(p, d).wait_recv()

    def tile_branch(first, n, s):
        total = None
        for side in range(2):
            cols = aligned(side * quarter + s * cw, cw)
            term = lax.dot_general(
                ubuf[aligned(first, rows, 16), cols],
                wbuf[aligned(n * 256, 256), cols],
                (((1,), (1,)), ((), ())),
                preferred_element_type=jnp.float32,
            )
            total = term if total is None else total + term
        return total

    def branch_part(s):
        w_ready(s)

        def body(t, _):
            first, n = (t // 4) * rows, t % 4
            place = (aligned(first, rows, 16), aligned(n * 256, 256))
            acc[place] += tile_branch(first, n, s)
            return 0

        lax.fori_loop(0, 2 * (feats // 256), body, 0)

    def b_sib(n):
        cols = aligned(n * 256, 256)
        return remote(bsend.at[:, cols], brecv.at[:, cols], b_sib_s.at[n], b_sib_r.at[n], sib)

    def b_out(n, j):
        yt = (y + j) % 4
        return remote(
            bout.at[aligned(yt * tok, tok, 16), aligned(n * 256, 256)],
            passed.at[:, aligned(y * feats + n * 256, 256)],
            b_out_s.at[n, j], b_out_r.at[n, j], at(x + 3, yt, z, c),
        )

    def branch_last(s):
        w_ready(s)

        def theirs(n, _):
            cols = aligned(n * 256, 256)
            bsend[:, cols] = (
                acc[aligned(oc * rows, rows, 16), cols] + tile_branch(oc * rows, n, s)
            ).astype(jnp.bfloat16)
            b_sib(n).start()
            return 0

        lax.fori_loop(0, feats // 256, theirs, 0)

        def ours(n, _):
            cols = aligned(n * 256, 256)
            total = acc[aligned(c * rows, rows, 16), cols] + tile_branch(c * rows, n, s)
            b_sib(n).wait_recv()
            bout[:, cols] = (total + brecv[:, cols].astype(jnp.float32)).astype(jnp.bfloat16)
            for j in range(4):
                b_out(n, j).start()
            return 0

        lax.fori_loop(0, feats // 256, ours, 0)

    chunks = 2 * subs
    c_local.start()

    def start_local(k, _):
        u_local(k).start()
        return 0

    lax.fori_loop(0, chunks, start_local, 0)
    pl.semaphore_wait(barrier, len(greet))
    c_opp.start()

    def start_sib(k, _):
        u_sib(k).start()
        return 0

    lax.fori_loop(0, chunks, start_sib, 0)
    for k in range(2):
        issue_own(k)
    lax.fori_loop(0, 16, clip_weights, 0)
    for p in range(2):
        for d in range(2):
            w_own(p, d).start()
    acc[...] = jnp.zeros_like(acc)
    c_local.wait()
    c_opp.wait_recv()
    c_sib.start()

    def pair(s, _):
        k = 2 * s
        y_stage(k)

        @pl.when(s == 1)
        def _():
            for d in range(2):
                w_own(3, d).start()

        @pl.when((s == 1) | (s == 2))
        def _():
            for d in range(2):
                w_own_wait = w_own(k - 2, d)
                w_own_wait.wait_recv()
                w_fwd(k - 2, d).start()

        @pl.when(s >= 1)
        def _():
            grad_side(s - 1)

        @pl.when(s >= 2)
        def _():
            combine(s - 2)

        y_stage(k + 1)

        @pl.when(s == 0)
        def _():
            for d in range(2):
                w_own(2, d).start()
            c_sib.wait_recv()
            lax.fori_loop(0, (2 * rows) // TILE, turn, 0)

        @pl.when((s == 1) | (s == 2))
        def _():
            for d in range(2):
                w_own(k - 1, d).wait_recv()
                w_fwd(k - 1, d).start()

        grad_same(s)

        @pl.when(s >= 1)
        def _():
            branch_part(s - 1)

        return 0

    lax.fori_loop(0, subs, pair, 0)
    grad_side(subs - 1)
    combine(subs - 2)
    branch_last(subs - 1)
    finish(0)
    finish(1)
    combine(subs - 1)
    finish(2)
    finish(3)

    c_opp.wait_send()
    c_sib.wait_send()

    def drain_u(k, _):
        u_sib(k).wait_send()
        for d in range(2):
            for cc in range(2):
                u_own_wait(k, d, cc).wait_send()
            u_fwd(k, d).wait_send()
        return 0

    lax.fori_loop(0, chunks, drain_u, 0)

    def drain(s, _):
        for d in range(2):
            w_own(s, d).wait_send()
            w_fwd(s, d).wait_send()
            g_half(s, d).wait_send()
            g_full(s, d).wait_send()
        b_sib(s).wait_send()
        for j in range(4):
            b_out(s, j).wait()
        master_copy(s).wait()
        return 0

    lax.fori_loop(0, subs, drain, 0)


def relay_call(up, picked, weight, noise, levels):
    tok, width = up.shape
    blk, quarter = weight.shape
    rows = 4 * tok
    brick, feats = 2 * rows, 2 * blk
    span = 2 * quarter
    cw = quarter // 4
    bf, f32 = jnp.bfloat16, jnp.float32
    dma = pltpu.SemaphoreType.DMA
    sems = [
        (8,), (8,), (8,), (8, 2, 2), (8, 2, 2), (8, 2), (8, 2),
        (1,), (1,), (1,), (1,), (1,),
        (4, 2), (4, 2), (4, 2), (4, 2),
        (4, 2), (4, 2), (4, 2), (4, 2),
        (4,), (4,), (4, 4), (4, 4), (4,),
    ]
    flops = 2 * 2 * brick * feats * span
    return pl.pallas_call(
        relay_kernel,
        out_shape=(jax.ShapeDtypeStruct((blk, quarter), f32), jax.ShapeDtypeStruct((tok, 4 * feats), bf)),
        in_specs=[
            pl.BlockSpec(memory_space=pl.ANY),
            pl.BlockSpec(memory_space=pl.ANY),
            pl.BlockSpec(memory_space=pltpu.VMEM),
            pl.BlockSpec(memory_space=pltpu.VMEM),
            pl.BlockSpec(memory_space=pltpu.SMEM),
        ],
        out_specs=(pl.BlockSpec(memory_space=pl.ANY), pl.BlockSpec(memory_space=pl.ANY)),
        scratch_shapes=[
            pltpu.VMEM((brick, span), bf),
            pltpu.VMEM((feats, span), bf),
            pltpu.VMEM((brick, feats), bf),
            pltpu.VMEM((feats, brick), bf),
            pltpu.VMEM((brick, feats), f32),
            pltpu.VMEM((blk, quarter), f32),
            pltpu.VMEM((4, blk, cw), bf),
            pltpu.VMEM((2, 4, blk, cw), bf),
            pltpu.VMEM((2, 4, blk // 2, cw), bf),
            pltpu.VMEM((2, 4, blk, cw), bf),
            pltpu.VMEM((rows, feats), bf),
            pltpu.VMEM((rows, feats), bf),
            pltpu.VMEM((rows, feats), bf),
        ]
        + [dma(shape) for shape in sems],
        compiler_params=pltpu.CompilerParams(
            collective_id=0, has_side_effects=True, vmem_limit_bytes=63 * 1024 * 1024
        ),
        cost_estimate=pl.CostEstimate(flops=flops, bytes_accessed=32 * 1024 * 1024, transcendentals=0),
        name="relay",
    )(up, picked, weight, noise, levels)


def local(upstream, saved_input, weight, weight_noise, levels, plan):
    section = lax.axis_index("pipe")
    tok = upstream.shape[1]
    blk = weight.shape[1]
    total_tokens = tok * lax.axis_size("tp") * lax.axis_size("dp")
    chosen = lax.dynamic_index_in_dim(saved_input[0], plan[section], 0, keepdims=False)
    picked = chosen.reshape(4, 2, tok, blk).transpose(1, 0, 2, 3).reshape(2, 4 * tok, blk)
    grad, arrived = relay_call(upstream[0], picked, weight[0], weight_noise[0], levels[0])
    master = grad * (1.0 / jnp.sqrt(jnp.float32(total_tokens)))
    last = section == lax.axis_size("pipe") - 1
    passed = jnp.where(last, jnp.zeros_like(arrived), arrived)
    return (master[None], passed[None])


def solution(mesh):
    placed = (
        P("pipe", ("dp", "tp"), None),
        P("pipe", None, "dp", "tp"),
        P("pipe", "tp", "dp"),
        P("pipe", "tp", "dp"),
        P("pipe", "tp", "dp"),
        P(),
    )
    return jax.shard_map(
        local,
        mesh=mesh,
        in_specs=placed,
        out_specs=(P("pipe", "tp", "dp"), P("pipe", ("dp", "tp"), None)),
        check_vma=False,
    )
```

time: 497 us -> 193 us (0.39)
  waiting for transfers between devices: 375 us -> 0 us
  Pallas kernels: 0 us -> 179 us
  matrix products: 43.6 us -> 0 us
  blocking collectives: 34.6 us -> 0 us
  between operations: 15.8 us -> 2.59 us
  other arithmetic: 14.8 us -> 6.26 us
    all_gather x2 -> x0, waiting for transfers between devices: 333 us -> none  [the longest x1 276 us: local(): grad_full = lax.all_gather(grad_in, 'tp', axis=0, tiled=True)]
    pallas_call x0 -> x1, Pallas kernels: none -> 179 us  [relay_call(): pl.pallas_call(relay_kernel, out_shape=(jax.ShapeDtypeStruct((blk, quarte...]
    dot_general x2 -> x0, matrix products: 43.6 us -> none  [the longest x1 22.6 us: local(): lax.dot_general(columns, chosen, (((0,), (0,)), ((), ())), preferred_elem...]
    ppermute x1 -> x0, waiting for transfers between devices: 35.5 us -> none  [shifted(): return lax.ppermute(block, axis, route)]
    all_to_all x1 -> x0, blocking collectives: 34.6 us -> none  [local(): lax.all_to_all(branch_out, 'tp', split_axis=0, concat_axis=1, tiled=True)]
    reduce_scatter x1 -> x0, waiting for transfers between devices: 5.31 us -> none  [local(): lax.psum_scatter(lax.dot_general(columns, chosen, (((0,), (0,)), ((), ())...]
  transfers between devices with their start and end apart: 4 -> 0, of which waited for: 4 -> 0; matrix products, arithmetic and copies ran while one was open for 11% -> 0% of each run, Pallas kernels for 0% -> 0%
where the time goes in v1:
time: 193 us; the launch traced here: 192 us
  Pallas kernels  179 us (93%)
  other arithmetic  6.26 us (3%)
  local copies, waits for them, and re-layouts  4.14 us (2%)
  between operations  2.59 us (1%)
    pallas_call x1, Pallas kernels, relay_call(): pl.pallas_call(relay_kernel, out_shape=(jax.ShapeDtypeStruct((blk, quarte...  179 us
    broadcast_in_dim x2, other arithmetic, local(): return (master[None], passed[None])  6.26 us

profile of v1, /device:TPU:6, one launch (start us, length us, event | category | flops | bytes accessed | tf_op | source)
XLA Modules:
  0.0 192.2 jit_solution(11390729175319851863)
XLA Ops:
  0.6 1.2 dynamic_slice.7
  3.8 1.6 constant_dynamic-slice_fusion
  5.4 1.3 copy.8
  6.7 179.2 %relay.1 = (f32[512,2048]{1,0:T(8,128)}, bf16[208,4096]{1,0:T(8,128)(2,1)}) custom-call(bf16[208,8192]{1,0:T(8,128)(2,1)} %bitcast.15, bf16[2,832,512]{2,1,0:T(8,128)(2,1)} %bitcast.14, bf16[512,2048]{1,0:T(8,128)(2,1)} %bitcast.16, bf16[512,2048]{1,0:T(8,128)(2,1)} %bitcast.17, s32[4,16]{1,0:T(4,128)} %bitcast.18), custom_call_target="tpu_custom_call" | custom-call | flops 27917287424 | bytes 33554432 | tf_op jit(solution)/shard_map/relay/pallas_call | solution.py:415
  185.9 1.3 select_bitcast_fusion
  187.2 5.0 %multiply_bitcast_fusion = f32[1,512,2048]{2,1,0:T(8,128)} fusion(f32[512,2048]{1,0:T(8,128)} %get-tuple-element.4), kind=kLoop, calls=%fused_computation | loop fusion | flops 1048576 | bytes 8388608 | tf_op jit(solution)/shard_map/broadcast_in_dim | solution.py:461

commit v2 on v1

v2 whole, which is shorter than its diff:
```python
import jax
import jax.numpy as jnp
from jax import lax
from jax.experimental import pallas as pl
from jax.experimental.pallas import tpu as pltpu
from jax.sharding import PartitionSpec as P

clip_step = 0.006
MESH = pl.DeviceIdType.MESH
TILE = 128


def aligned(start, size, step=128):
    return pl.ds(pl.multiple_of(start, step), size)


def relay_kernel(
    up, saved, weight_in, noise_in, levels, plan,
    master, passed,
    ubuf, wbuf, cbuf, ctbuf, acc, gbuf, ghalf, gfull, ready, bsend, brecv, bout, weight, noise,
    u_loc, u_sib_s, u_sib_r, u_own_s, u_own_r, u_fwd_s, u_fwd_r,
    c_loc, c_opp_s, c_opp_r, c_sib_s, c_sib_r,
    w_loc, w_own_s, w_own_r, w_fwd_s, w_fwd_r,
    g_half_s, g_half_r, g_full_s, g_full_r,
    b_sib_s, b_sib_r, b_out_s, b_out_r, m_out,
):
    tok = up.shape[0]
    rows = tok * 4
    near, far = 3 * tok, tok
    quarter = weight.shape[1]
    blk = weight.shape[0]
    half = blk // 2
    subs = 4
    chunks = 2 * subs
    cw = quarter // subs
    tiles = cw // TILE
    feats = 2 * blk
    ahead = 4

    x = lax.axis_index("pipe")
    tp = lax.axis_index("tp")
    dp = lax.axis_index("dp")
    y, zh = tp // 2, tp % 2
    zl, c = dp // 2, dp % 2
    z = 2 * zh + zl
    oc = 1 - c

    def at(xx, yy, zz, cc):
        xx, yy, zz = xx % 4, yy % 4, zz % 4
        return (xx, yy * 2 + zz // 2, (zz % 2) * 2 + cc)

    sib = at(x, y, z, oc)
    opp = at(x, y, z + 2, c)
    ynb = (at(x, y + 1, z, c), at(x, y + 3, z, c))
    znb = (at(x, y, z + 1, c), at(x, y, z + 3, c))
    zp = (zh + zl) % 2
    zside = (zp, 1 - zp)

    barrier = pltpu.get_barrier_semaphore()
    greet = [sib, opp, *ynb, *znb] + [at(x + 1, y + j, z, c) for j in range(4)]
    for one in greet:
        pl.semaphore_signal(barrier, inc=1, device_id=one, device_id_type=MESH)

    def remote(src, dst, s, r, to):
        return pltpu.make_async_remote_copy(
            src_ref=src, dst_ref=dst, send_sem=s, recv_sem=r, device_id=to, device_id_type=MESH
        )

    def each(count, body):
        def one(i, _):
            body(i)
            return 0

        lax.fori_loop(0, count, one, 0)

    def near_rows(cc):
        return aligned(cc * near, near, 16)

    def far_rows(cc):
        return aligned(2 * near + cc * far, far, 16)

    def row(slot, cc):
        return aligned(cc * near + slot * tok, tok, 16)

    def ucol(k):
        return aligned((k % 2) * quarter + (k // 2) * cw, cw)

    def hcol(k, cc):
        return aligned(((zl + k) % 2) * (2 * quarter) + cc * quarter + (k // 2) * cw, cw)

    def u_local(k):
        return pltpu.make_async_copy(up.at[:, hcol(k, c)], ubuf.at[row(0, c), ucol(k)], u_loc.at[k])

    def u_sib(k):
        return remote(up.at[:, hcol(k, oc)], ubuf.at[row(0, c), ucol(k)], u_sib_s.at[k], u_sib_r.at[k], sib)

    def u_own(k, d, mine):
        cc = c if mine else oc
        src = up.at[:, hcol(k, c)] if mine else ubuf.at[row(0, oc), ucol(k)]
        return remote(src, ubuf.at[row(2 - d, cc), ucol(k)], u_own_s.at[k, d, cc], u_own_r.at[k, d, cc], ynb[d])

    def u_own_wait(k, d, cc):
        ref = ubuf.at[row(2 - d, cc), ucol(k)]
        return remote(ref, ref, u_own_s.at[k, d, cc], u_own_r.at[k, d, cc], ynb[d])

    def u_fwd(k, d):
        return remote(
            ubuf.at[row(2 - d, d), ucol(k)], ubuf.at[far_rows(d), ucol(k)], u_fwd_s.at[k, d], u_fwd_r.at[k, d], ynb[d]
        )

    def own_mine(k):
        for d in range(2):
            u_own(k, d, True).start()

    def own_theirs(k):
        u_sib(k).wait_recv()
        for d in range(2):
            u_own(k, d, False).start()

    def pass_on(k):
        for d in range(2):
            u_fwd(k, d).start()

    def w_load(p):
        place = aligned(p * cw, cw)
        return [
            pltpu.make_async_copy(weight_in.at[:, place], weight.at[:, place], w_loc.at[p, 0]),
            pltpu.make_async_copy(noise_in.at[:, place], noise.at[:, place], w_loc.at[p, 1]),
        ]

    def wref(hi, first, count, side, p):
        return wbuf.at[aligned(hi * blk + first, count), aligned(side * quarter + p * cw, cw)]

    def w_own(p, d):
        return remote(wref(zh, 0, blk, 0, p), wref(zh, 0, blk, 1, p), w_own_s.at[p, d], w_own_r.at[p, d], znb[d])

    def w_fwd(p, d):
        hi = zside[1 - d]
        return remote(
            wref(hi, d * half, half, 1, p), wref(hi, d * half, half, 0, p), w_fwd_s.at[p, d], w_fwd_r.at[p, d], znb[d]
        )

    def w_pass_on(p):
        for d in range(2):
            w_own(p, d).wait_recv()
            w_fwd(p, d).start()

    def clip_weights(p):
        for one in w_load(p):
            one.wait()

        def body(i):
            for j in range(tiles):
                bound = levels[i, p * tiles + j].astype(jnp.float32) * clip_step
                place = (aligned(i * TILE, TILE), aligned(p * cw + j * TILE, TILE))
                noisy = weight[place].astype(jnp.float32) + noise[place].astype(jnp.float32)
                wbuf[aligned(zh * blk + i * TILE, TILE), aligned(p * cw + j * TILE, TILE)] = jnp.minimum(
                    jnp.maximum(noisy, -bound), bound
                ).astype(jnp.bfloat16)

        each(blk // TILE, body)

    def c_load(t):
        slot, other = t // 2, t % 2
        rel = (0, 1, 3, 2)[slot]
        place = (pl.ds(slot * tok, tok), pl.ds(other * blk, blk))
        src = ((y + rel) % 4, (zh + other) % 2)
        return [
            pltpu.make_async_copy(saved.at[(0, *src)], bsend.at[place], c_loc.at[t, 0]),
            pltpu.make_async_copy(saved.at[(1, *src)], bout.at[place], c_loc.at[t, 1]),
        ]

    def ccol(hi):
        return aligned(hi * blk, blk)

    def c_opp(part):
        src = (pl.ds(0, near), pl.ds(near, far))[part]
        dst = (near_rows(c), far_rows(c))[part]
        return remote(
            bout.at[src, pl.ds(blk, blk)], cbuf.at[dst, ccol(zh)], c_opp_s.at[part], c_opp_r.at[part], opp
        )

    def c_sib(part):
        ref = cbuf.at[(near_rows(c), far_rows(c))[part]]
        return remote(ref, ref, c_sib_s.at[part], c_sib_r.at[part], sib)

    def pick_batch():
        for t in range(8):
            for one in c_load(t):
                one.wait()
        second = plan[x].astype(jnp.float32)
        first = 1.0 - second

        def picked(place):
            return (
                bsend[place].astype(jnp.float32) * first + bout[place].astype(jnp.float32) * second
            ).astype(jnp.bfloat16)

        for slot in range(4):
            begin = c * near + slot * tok if slot < 3 else 2 * near + c * far

            def body(i):
                src = aligned(slot * tok + i * 16, 16, 16)
                cbuf[aligned(begin + i * 16, 16, 16), ccol(zh)] = picked((src, pl.ds(0, blk)))
                other = (src, pl.ds(blk, blk))
                bout[other] = picked(other)

            each(tok // 16, body)

    def turn(t):
        place = aligned(t * TILE, TILE)
        ctbuf[:, place] = cbuf[place, :].T

    def grad_chunk(k):
        for d in range(2):
            u_fwd(k, d).wait_recv()

        def body(t):
            b, n = t // 2, t % 2
            hi = (b + zh + (k % 2) * zl) % 2
            cols = aligned((k % 2) * quarter + (k // 2) * cw + n * 256, 256)
            gbuf[k, b, :, aligned(n * 256, 256)] = jnp.dot(
                ctbuf[aligned(hi * blk, blk), :], ubuf[:, cols], preferred_element_type=jnp.float32
            ).astype(jnp.bfloat16)

        each(4, body)

        @pl.when(k % 2 == 0)
        def _():
            for d in range(2):
                g_half(k // 2, d).start()

    def g_half(s, d):
        return remote(
            gbuf.at[2 * s, 1, pl.ds(d * half, half)], ghalf.at[d, s], g_half_s.at[s, d], g_half_r.at[s, d], znb[d]
        )

    def g_full(s, d):
        return remote(gbuf.at[2 * s + 1, d], gfull.at[d, s], g_full_s.at[s, d], g_full_r.at[s, d], znb[d])

    def combine(s):
        for d in range(2):
            g_half(s, d).wait_recv()
            for i in range(half // 64):
                inner = pl.ds(i * 64, 64)
                place = pl.ds(d * half + i * 64, 64)
                gbuf[2 * s + 1, d, place] = (
                    gbuf[2 * s + 1, d, place].astype(jnp.float32) + ghalf[d, s, inner].astype(jnp.float32)
                ).astype(jnp.bfloat16)
            g_full(s, d).start()

    def master_copy(s):
        return pltpu.make_async_copy(ready.at[s], master.at[:, aligned(s * cw, cw)], m_out.at[s])

    def finish(s):
        for d in range(2):
            g_full(s, d).wait_recv()
        scale = 1.0 / (float(rows) * 8.0) ** 0.5

        def body(i):
            line = aligned(i * TILE, TILE)
            for j in range(tiles):
                bound = levels[i, s * tiles + j].astype(jnp.float32) * clip_step
                place = (line, aligned(s * cw + j * TILE, TILE))
                noisy = weight[place].astype(jnp.float32) + noise[place].astype(jnp.float32)
                inner = pl.ds(j * TILE, TILE)
                total = gbuf[2 * s, 0, line, inner].astype(jnp.float32) + gfull[0, s, line, inner].astype(jnp.float32)
                total = total + gfull[1, s, line, inner].astype(jnp.float32)
                ready[s, line, inner] = jnp.where(jnp.abs(noisy) <= bound, total * scale, 0.0)

        each(blk // TILE, body)
        master_copy(s).start()

    def w_ready(p):
        for d in range(2):
            w_fwd(p, d).wait_recv()

    def tile_branch(place, n, sides):
        total = None
        for cols in sides:
            term = lax.dot_general(
                ubuf[place, cols],
                wbuf[aligned(n * 256, 256), cols],
                (((1,), (1,)), ((), ())),
                preferred_element_type=jnp.float32,
            )
            total = term if total is None else total + term
        return total

    def branch_near(s):
        w_ready(s)
        sides = [aligned(side * quarter + s * cw, cw) for side in range(2)]

        def body(t):
            place, cols = near_rows(t // 4), aligned((t % 4) * 256, 256)
            acc[place, cols] += tile_branch(place, t % 4, sides)

        each(2 * (feats // 256), body)

    def b_sib(part, n):
        place = ((pl.ds(0, near), pl.ds(near, far))[part], aligned(n * 256, 256))
        return remote(bsend.at[place], brecv.at[place], b_sib_s.at[part, n], b_sib_r.at[part, n], sib)

    def b_out(n, slot):
        yt = (y + (0, 1, 3, 2)[slot]) % 4
        return remote(
            bout.at[pl.ds(slot * tok, tok), aligned(n * 256, 256)],
            passed.at[:, aligned(y * feats + n * 256, 256)],
            b_out_s.at[n, slot], b_out_r.at[n, slot], at(x + 3, yt, z, c),
        )

    def branch_send(part, first, count, slots):
        def place(cc):
            return aligned(cc * count, count, 16)

        def theirs(n):
            cols = aligned(n * 256, 256)
            bsend[pl.ds(first, count), cols] = acc[place(oc), cols].astype(jnp.bfloat16)
            b_sib(part, n).start()

        each(feats // 256, theirs)

        def ours(n):
            cols = aligned(n * 256, 256)
            b_sib(part, n).wait_recv()
            total = acc[place(c), cols] + brecv[pl.ds(first, count), cols].astype(jnp.float32)
            bout[pl.ds(first, count), cols] = jnp.where(x == 0, 0.0, total).astype(jnp.bfloat16)
            for slot in slots:
                b_out(n, slot).start()

        each(feats // 256, ours)

    def branch_far():
        whole = pl.ds(2 * near, 2 * far)

        def body(n):
            acc[pl.ds(0, 2 * far), aligned(n * 256, 256)] = tile_branch(
                whole, n, [pl.ds(i * quarter, quarter) for i in range(2)]
            )

        each(feats // 256, body)

    for p in range(subs):
        for one in w_load(p):
            one.start()
    for t in range(8):
        for one in c_load(t):
            one.start()
    each(chunks, lambda k: u_local(k).start())
    each(subs, clip_weights)
    pl.semaphore_wait(barrier, len(greet))
    for k in range(2):
        u_sib(k).start()
        own_mine(k)
    for p in range(2):
        for d in range(2):
            w_own(p, d).start()
    each(chunks - 2, lambda k: u_sib(k + 2).start())
    for k in range(2):
        own_theirs(k)
    pick_batch()
    for part in range(2):
        c_opp(part).start()
    for p in range(2, 4):
        for d in range(2):
            w_own(p, d).start()
    acc[...] = jnp.zeros_like(acc)

    def step(k):
        @pl.when(k < chunks)
        def _():
            for d in range(2):
                u_own_wait(k, d, d).wait_recv()

            @pl.when(k >= ahead - 1)
            def _():
                pass_on(k - (ahead - 1))

            @pl.when(k + 2 < chunks)
            def _():
                own_mine(k + 2)
                own_theirs(k + 2)

            @pl.when(k == chunks - 1)
            def _():
                each(ahead - 1, lambda i: pass_on(chunks - ahead + 1 + i))

            u_local(k).wait()
            for d in range(2):
                u_own_wait(k, d, 1 - d).wait_recv()

        @pl.when(k < 2)
        def _():
            w_pass_on(k)

        @pl.when(k == 3)
        def _():
            for part in range(2):
                c_opp(part).wait_recv()
                c_sib(part).start()
            for part in range(2):
                c_sib(part).wait_recv()
            each((2 * rows) // TILE, turn)

        @pl.when(k >= ahead)
        def _():
            grad_chunk(k - ahead)

        @pl.when((k == 4) | (k == 5))
        def _():
            w_pass_on(k - 2)

        @pl.when((k >= 4) & (k < 8))
        def _():
            branch_near(k - 4)

        @pl.when(k == 7)
        def _():
            for part in range(2):
                c_opp(part).wait_send()
            branch_send(0, 0, near, (0, 1, 2))

        @pl.when((k == 6) | (k == 8))
        def _():
            combine((k - 6) // 2)

    each(chunks + ahead, step)
    branch_far()
    branch_send(1, near, far, (3,))
    combine(2)
    finish(0)
    finish(1)
    combine(3)
    finish(2)
    finish(3)

    for part in range(2):
        c_sib(part).wait_send()

    def drain_u(k):
        u_sib(k).wait_send()
        for d in range(2):
            for cc in range(2):
                u_own_wait(k, d, cc).wait_send()
            u_fwd(k, d).wait_send()

    each(chunks, drain_u)

    def drain(s):
        for d in range(2):
            w_own(s, d).wait_send()
            w_fwd(s, d).wait_send()
            g_half(s, d).wait_send()
            g_full(s, d).wait_send()
        for part in range(2):
            b_sib(part, s).wait_send()
        for slot in range(4):
            b_out(s, slot).wait()
        master_copy(s).wait()

    each(subs, drain)


def relay_call(up, saved, weight, noise, levels, plan):
    tok, width = up.shape
    blk, quarter = weight.shape
    rows = 4 * tok
    brick, feats = 2 * rows, 2 * blk
    span = 2 * quarter
    cw = quarter // 4
    bf, f32 = jnp.bfloat16, jnp.float32
    dma = pltpu.SemaphoreType.DMA
    sems = [
        (8,), (8,), (8,), (8, 2, 2), (8, 2, 2), (8, 2), (8, 2),
        (8, 2), (2,), (2,), (2,), (2,),
        (4, 2), (4, 2), (4, 2), (4, 2), (4, 2),
        (4, 2), (4, 2), (4, 2), (4, 2),
        (2, 4), (2, 4), (4, 4), (4, 4), (4,),
    ]
    flops = 2 * 2 * brick * feats * span
    anywhere = pl.BlockSpec(memory_space=pl.ANY)
    scalars = pl.BlockSpec(memory_space=pltpu.SMEM)
    return pl.pallas_call(
        relay_kernel,
        out_shape=(jax.ShapeDtypeStruct((blk, quarter), f32), jax.ShapeDtypeStruct((tok, 4 * feats), bf)),
        in_specs=[anywhere, anywhere, anywhere, anywhere, scalars, scalars],
        out_specs=(anywhere, anywhere),
        scratch_shapes=[
            pltpu.VMEM((brick, span), bf),
            pltpu.VMEM((feats, span), bf),
            pltpu.VMEM((brick, feats), bf),
            pltpu.VMEM((feats, brick), bf),
            pltpu.VMEM((6 * tok, feats), f32),
            pltpu.VMEM((8, 2, blk, cw), bf),
            pltpu.VMEM((2, 4, blk // 2, cw), bf),
            pltpu.VMEM((2, 4, blk, cw), bf),
            pltpu.VMEM((4, blk, cw), f32),
            pltpu.VMEM((rows, feats), bf),
            pltpu.VMEM((rows, feats), bf),
            pltpu.VMEM((rows, feats), bf),
            pltpu.VMEM((blk, quarter), bf),
            pltpu.VMEM((blk, quarter), bf),
        ]
        + [dma(shape) for shape in sems],
        compiler_params=pltpu.CompilerParams(
            collective_id=0, has_side_effects=True, vmem_limit_bytes=63 * 1024 * 1024
        ),
        cost_estimate=pl.CostEstimate(flops=flops, bytes_accessed=32 * 1024 * 1024, transcendentals=0),
        name="relay",
    )(up, saved, weight, noise, levels, plan)


def hand_over(grad, arrived):
    parts = 8
    pieces = []
    for which, one in enumerate((grad, arrived)):
        many = parts if one.shape[0] % (parts * 16) == 0 else 1
        size = one.shape[0] // many
        pieces += [(which, pl.ds(i * size, size)) for i in range(many)]

    def kernel(grad_in, arrived_in, grad_out, arrived_out, grad_held, arrived_held, load_sem, store_sem):
        routes = ((grad_in, grad_held, grad_out), (arrived_in, arrived_held, arrived_out))
        loads, stores = [], []
        for i, (which, place) in enumerate(pieces):
            src, held, dst = (ref.at[place] for ref in routes[which])
            loads.append(pltpu.make_async_copy(src, held, load_sem.at[i]))
            stores.append(pltpu.make_async_copy(held, dst, store_sem.at[i]))
        for one in loads:
            one.start()
        for load, store in zip(loads, stores):
            load.wait()
            store.start()
        for one in stores:
            one.wait()

    anywhere = pl.BlockSpec(memory_space=pl.ANY)
    return pl.pallas_call(
        kernel,
        out_shape=tuple(jax.ShapeDtypeStruct(one.shape, one.dtype) for one in (grad, arrived)),
        in_specs=[anywhere, anywhere],
        out_specs=(anywhere, anywhere),
        scratch_shapes=[pltpu.VMEM(one.shape, one.dtype) for one in (grad, arrived)]
        + [pltpu.SemaphoreType.DMA((len(pieces),)), pltpu.SemaphoreType.DMA((len(pieces),))],
        compiler_params=pltpu.CompilerParams(vmem_limit_bytes=63 * 1024 * 1024),
        name="hand_over",
    )(grad, arrived)


def local(upstream, saved_input, weight, weight_noise, levels, plan):
    tok = upstream.shape[1]
    blk = weight.shape[1]
    saved = saved_input.reshape(saved_input.shape[1], 4, 2, tok, blk)
    grad, arrived = relay_call(upstream[0], saved, weight[0], weight_noise[0], levels[0], plan)
    master, passed = hand_over(grad, arrived)
    return (master[None], passed[None])


def solution(mesh):
    placed = (
        P("pipe", ("dp", "tp"), None),
        P("pipe", None, "dp", "tp"),
        P("pipe", "tp", "dp"),
        P("pipe", "tp", "dp"),
        P("pipe", "tp", "dp"),
        P(),
    )
    return jax.shard_map(
        local,
        mesh=mesh,
        in_specs=placed,
        out_specs=(P("pipe", "tp", "dp"), P("pipe", ("dp", "tp"), None)),
        check_vma=False,
    )
```

time: 193 us -> 175 us (0.907)
  the two profiles are of different devices: /device:TPU:6 before, /device:TPU:1 now
where the time goes in v2:
time: 175 us
  Pallas kernels  174 us (99%)
    pallas_call x1, Pallas kernels, relay_call(): pl.pallas_call(relay_kernel, out_shape=(jax.ShapeDtypeStruct((blk, quarte...  169 us
    pallas_call x1, Pallas kernels, hand_over(): pl.pallas_call(kernel, out_shape=tuple((jax.ShapeDtypeStruct(one.shape, o...  5.59 us

profile of v2, /device:TPU:1, one launch (start us, length us, event | category | flops | bytes accessed | tf_op | source)
XLA Modules:
  0.0 174.8 jit_solution(8156934448042401252)
XLA Ops:
  0.6 168.6 %relay.1 = (f32[512,2048]{1,0:T(8,128)}, bf16[208,4096]{1,0:T(8,128)(2,1)}) custom-call(bf16[208,8192]{1,0:T(8,128)(2,1)} %bitcast.8, bf16[2,4,2,208,512]{4,3,2,1,0:T(8,128)(2,1)} %bitcast.9, bf16[512,2048]{1,0:T(8,128)(2,1)} %bitcast.10, bf16[512,2048]{1,0:T(8,128)(2,1)} %bitcast.11, s32[4,16]{1,0:T(4,128)} %bitcast.13, s32[4]{0:T(128)} %plan.1), custom_call_target="tpu_custom_call" | custom-call | flops 27917287424 | bytes 33554432 | tf_op jit(solution)/shard_map/relay/pallas_call | solution.py:483
  169.2 5.6 %hand_over.1 = (f32[512,2048]{1,0:T(8,128)}, bf16[208,4096]{1,0:T(8,128)(2,1)}) custom-call(f32[512,2048]{1,0:T(8,128)} %get-tuple-element.6.grad_in, bf16[208,4096]{1,0:T(8,128)(2,1)} %get-tuple-element.7.arrived_in), custom_call_target="tpu_custom_call" | custom-call | tf_op jit(solution)/shard_map/hand_over/pallas_call | solution.py:537

commit v3 on v2

--- a/solution.py
+++ b/solution.py
@@ -20,7 +20,7 @@
     ubuf, wbuf, cbuf, ctbuf, acc, gbuf, ghalf, gfull, ready, bsend, brecv, bout, weight, noise,
     u_loc, u_sib_s, u_sib_r, u_own_s, u_own_r, u_fwd_s, u_fwd_r,
     c_loc, c_opp_s, c_opp_r, c_sib_s, c_sib_r,
-    w_loc, w_own_s, w_own_r, w_fwd_s, w_fwd_r,
+    w_loc, w_own_s, w_own_r, w_leaf_s, w_leaf_r, w_fwd_s, w_fwd_r, w_off_s, w_off_r,
     g_half_s, g_half_r, g_full_s, g_full_r,
     b_sib_s, b_sib_r, b_out_s, b_out_r, m_out,
 ):
@@ -35,7 +35,7 @@
     cw = quarter // subs
     tiles = cw // TILE
     feats = 2 * blk
-    ahead = 4
+    ahead = 3
 
     x = lax.axis_index("pipe")
     tp = lax.axis_index("tp")
@@ -61,6 +61,18 @@
     for one in greet:
         pl.semaphore_signal(barrier, inc=1, device_id=one, device_id_type=MESH)
 
+    @pl.when(x > 0)
+    def _():
+        pl.semaphore_signal(barrier, inc=1, device_id=at(0, y, z, c), device_id_type=MESH)
+
+    @pl.when(x == 0)
+    def _():
+        for plane in range(1, 4):
+            for step in (1, 3):
+                pl.semaphore_signal(barrier, inc=1, device_id=at(plane, y, z + step, c), device_id_type=MESH)
+
+    greeted = len(greet) + 3 - (x + 3) // 4
+
     def remote(src, dst, s, r, to):
         return pltpu.make_async_remote_copy(
             src_ref=src, dst_ref=dst, send_sem=s, recv_sem=r, device_id=to, device_id_type=MESH
@@ -132,7 +144,35 @@
         return wbuf.at[aligned(hi * blk + first, count), aligned(side * quarter + p * cw, cw)]
 
     def w_own(p, d):
-        return remote(wref(zh, 0, blk, 0, p), wref(zh, 0, blk, 1, p), w_own_s.at[p, d], w_own_r.at[p, d], znb[d])
+        return remote(
+            wref(zh, d * half, half, 0, p), wref(zh, d * half, half, 1, p), w_own_s.at[p, d], w_own_r.at[p, d], znb[d]
+        )
+
+    def w_leaf(p, d):
+        first = (1 - d) * half
+        return remote(
+            wref(zh, first, half, 0, p), wref(zh, first, half, 1, p), w_leaf_s.at[p, d], w_leaf_r.at[p, d], znb[d]
+        )
+
+    def held(plane, d, u):
+        i = ((plane - 1) * 2 + d) * 2 + u
+        return wbuf.at[aligned((i // 8) * half, half), aligned((i % 8) * cw, cw)]
+
+    def w_off(d, u):
+        to = at(0, y, z + 1 + 2 * d, c)
+        return remote(
+            wref(zh, (1 - d) * half, half, 0, u + 2), held(x, d, u), w_leaf_s.at[u + 2, d], w_off_r.at[x - 1, d, u], to
+        )
+
+    def w_back(plane, d, u):
+        dst = wref(zside[1 - d], (1 - d) * half, half, 1, u + 2)
+        return remote(
+            held(plane, d, u), dst, w_off_s.at[plane - 1, d, u], w_leaf_r.at[u + 2, d], at(plane, y, z, c)
+        )
+
+    def w_off_wait(plane, d, u):
+        ref = held(plane, d, u)
+        return remote(ref, ref, w_off_s.at[plane - 1, d, u], w_off_r.at[plane - 1, d, u], sib)
 
     def w_fwd(p, d):
         hi = zside[1 - d]
@@ -149,6 +189,11 @@
         for one in w_load(p):
             one.wait()
 
+        @pl.when(x > 0)
+        def _():
+            clip_columns(p)
+
+    def clip_columns(p):
         def body(i):
             for j in range(tiles):
                 bound = levels[i, p * tiles + j].astype(jnp.float32) * clip_step
@@ -273,6 +318,7 @@
 
     def w_ready(p):
         for d in range(2):
+            w_leaf(p, d).wait_recv()
             w_fwd(p, d).wait_recv()
 
     def tile_branch(place, n, sides):
@@ -318,17 +364,30 @@
             bsend[pl.ds(first, count), cols] = acc[place(oc), cols].astype(jnp.bfloat16)
             b_sib(part, n).start()
 
-        each(feats // 256, theirs)
-
         def ours(n):
             cols = aligned(n * 256, 256)
             b_sib(part, n).wait_recv()
             total = acc[place(c), cols] + brecv[pl.ds(first, count), cols].astype(jnp.float32)
-            bout[pl.ds(first, count), cols] = jnp.where(x == 0, 0.0, total).astype(jnp.bfloat16)
+            bout[pl.ds(first, count), cols] = total.astype(jnp.bfloat16)
+
+        def send(n):
             for slot in slots:
                 b_out(n, slot).start()
 
-        each(feats // 256, ours)
+        @pl.when(x > 0)
+        def _():
+            each(feats // 256, theirs)
+
+            def both(n):
+                ours(n)
+                send(n)
+
+            each(feats // 256, both)
+
+        @pl.when(x == 0)
+        def _():
+            bout[pl.ds(first, count), :] = jnp.zeros((count, feats), jnp.bfloat16)
+            each(feats // 256, send)
 
     def branch_far():
         whole = pl.ds(2 * near, 2 * far)
@@ -348,22 +407,27 @@
             one.start()
     each(chunks, lambda k: u_local(k).start())
     each(subs, clip_weights)
-    pl.semaphore_wait(barrier, len(greet))
+    pl.semaphore_wait(barrier, greeted)
     for k in range(2):
         u_sib(k).start()
         own_mine(k)
-    for p in range(2):
-        for d in range(2):
-            w_own(p, d).start()
+
+    pick_batch()
+    for part in range(2):
+        c_opp(part).start()
+
+    @pl.when(x > 0)
+    def _():
+        for u in range(2):
+            for d in range(2):
+                w_off(d, u).start()
+        for d in range(2):
+            w_own(0, d).start()
+            w_leaf(0, d).start()
+
     each(chunks - 2, lambda k: u_sib(k + 2).start())
     for k in range(2):
         own_theirs(k)
-    pick_batch()
-    for part in range(2):
-        c_opp(part).start()
-    for p in range(2, 4):
-        for d in range(2):
-            w_own(p, d).start()
     acc[...] = jnp.zeros_like(acc)
 
     def step(k):
@@ -389,9 +453,29 @@
             for d in range(2):
                 u_own_wait(k, d, 1 - d).wait_recv()
 
-        @pl.when(k < 2)
-        def _():
-            w_pass_on(k)
+        @pl.when((x == 0) & ((k == 2) | (k == 4)))
+        def _():
+            u = (k - 2) // 2
+            for plane in (1, 3, 2):
+                for d in range(2):
+                    w_off_wait(plane, d, u).wait_recv()
+                    w_back(plane, d, u).start()
+
+        @pl.when((x > 0) & (k == 1))
+        def _():
+            w_pass_on(0)
+
+        @pl.when((x > 0) & (k == 2))
+        def _():
+            for d in range(2):
+                w_own(1, d).start()
+                w_leaf(1, d).start()
+                w_own(2, d).start()
+
+        @pl.when((x > 0) & (k == 3))
+        def _():
+            for d in range(2):
+                w_own(3, d).start()
 
         @pl.when(k == 3)
         def _():
@@ -402,35 +486,44 @@
                 c_sib(part).wait_recv()
             each((2 * rows) // TILE, turn)
 
-        @pl.when(k >= ahead)
+        @pl.when((x > 0) & (k == 4))
+        def _():
+            w_pass_on(1)
+            w_pass_on(2)
+
+        @pl.when((x > 0) & (k == 5))
+        def _():
+            w_pass_on(3)
+
+        @pl.when((k >= ahead) & (k != 7))
         def _():
             grad_chunk(k - ahead)
 
-        @pl.when((k == 4) | (k == 5))
-        def _():
-            w_pass_on(k - 2)
-
-        @pl.when((k >= 4) & (k < 8))
+        @pl.when((x > 0) & (k >= 4) & (k < 8))
         def _():
             branch_near(k - 4)
+
+        @pl.when((k == 5) | (k == 7) | (k == 9))
+        def _():
+            combine((k - 5) // 2)
 
         @pl.when(k == 7)
         def _():
             for part in range(2):
                 c_opp(part).wait_send()
             branch_send(0, 0, near, (0, 1, 2))
-
-        @pl.when((k == 6) | (k == 8))
-        def _():
-            combine((k - 6) // 2)
+            grad_chunk(k - ahead)
 
     each(chunks + ahead, step)
-    branch_far()
+
+    @pl.when(x > 0)
+    def _():
+        branch_far()
+
     branch_send(1, near, far, (3,))
-    combine(2)
+    combine(3)
     finish(0)
     finish(1)
-    combine(3)
     finish(2)
     finish(3)
 
@@ -448,17 +541,30 @@
 
     def drain(s):
         for d in range(2):
-            w_own(s, d).wait_send()
-            w_fwd(s, d).wait_send()
             g_half(s, d).wait_send()
             g_full(s, d).wait_send()
-        for part in range(2):
-            b_sib(part, s).wait_send()
+
+        @pl.when(x > 0)
+        def _():
+            for d in range(2):
+                w_own(s, d).wait_send()
+                w_leaf(s, d).wait_send()
+                w_fwd(s, d).wait_send()
+            for part in range(2):
+                b_sib(part, s).wait_send()
+
         for slot in range(4):
             b_out(s, slot).wait()
         master_copy(s).wait()
 
     each(subs, drain)
+
+    @pl.when(x == 0)
+    def _():
+        for plane in range(1, 4):
+            for d in range(2):
+                for u in range(2):
+                    w_back(plane, d, u).wait_send()
 
 
 def relay_call(up, saved, weight, noise, levels, plan):
@@ -473,7 +579,7 @@
     sems = [
         (8,), (8,), (8,), (8, 2, 2), (8, 2, 2), (8, 2), (8, 2),
         (8, 2), (2,), (2,), (2,), (2,),
-        (4, 2), (4, 2), (4, 2), (4, 2), (4, 2),
+        (4, 2), (4, 2), (4, 2), (4, 2), (4, 2), (4, 2), (4, 2), (3, 2, 2), (3, 2, 2),
         (4, 2), (4, 2), (4, 2), (4, 2),
         (2, 4), (2, 4), (4, 4), (4, 4), (4,),
     ]

time: 175 us -> 165 us (0.943)
  the two profiles are of different devices: /device:TPU:1 before, /device:TPU:6 now
where the time goes in v3:
time: 165 us
  Pallas kernels  164 us (99%)
    pallas_call x1, Pallas kernels, relay_call(): pl.pallas_call(relay_kernel, out_shape=(jax.ShapeDtypeStruct((blk, quarte...  159 us
    pallas_call x1, Pallas kernels, hand_over(): pl.pallas_call(kernel, out_shape=tuple((jax.ShapeDtypeStruct(one.shape, o...  5.59 us

profile of v3, /device:TPU:6, one launch (start us, length us, event | category | flops | bytes accessed | tf_op | source)
XLA Modules:
  0.0 164.7 jit_solution(17539558106924698610)
XLA Ops:
  0.6 158.5 %relay.1 = (f32[512,2048]{1,0:T(8,128)}, bf16[208,4096]{1,0:T(8,128)(2,1)}) custom-call(bf16[208,8192]{1,0:T(8,128)(2,1)} %bitcast.8, bf16[2,4,2,208,512]{4,3,2,1,0:T(8,128)(2,1)} %bitcast.9, bf16[512,2048]{1,0:T(8,128)(2,1)} %bitcast.10, bf16[512,2048]{1,0:T(8,128)(2,1)} %bitcast.11, s32[4,16]{1,0:T(4,128)} %bitcast.13, s32[4]{0:T(128)} %plan.1), custom_call_target="tpu_custom_call" | custom-call | flops 27917287424 | bytes 33554432 | tf_op jit(solution)/shard_map/relay/pallas_call | solution.py:589
  159.1 5.6 %hand_over.1 = (f32[512,2048]{1,0:T(8,128)}, bf16[208,4096]{1,0:T(8,128)(2,1)}) custom-call(f32[512,2048]{1,0:T(8,128)} %get-tuple-element.6.grad_in, bf16[208,4096]{1,0:T(8,128)(2,1)} %get-tuple-element.7.arrived_in), custom_call_target="tpu_custom_call" | custom-call | tf_op jit(solution)/shard_map/hand_over/pallas_call | solution.py:643

commit v4 on v3

--- a/solution.py
+++ b/solution.py
@@ -280,8 +280,11 @@
             gbuf.at[2 * s, 1, pl.ds(d * half, half)], ghalf.at[d, s], g_half_s.at[s, d], g_half_r.at[s, d], znb[d]
         )
 
-    def g_full(s, d):
-        return remote(gbuf.at[2 * s + 1, d], gfull.at[d, s], g_full_s.at[s, d], g_full_r.at[s, d], znb[d])
+    def g_full(s, d, h):
+        place = pl.ds(h * half, half)
+        return remote(
+            gbuf.at[2 * s + 1, d, place], gfull.at[d, s, place], g_full_s.at[s, d, h], g_full_r.at[s, d, h], znb[d]
+        )
 
     def combine(s):
         for d in range(2):
@@ -292,14 +295,16 @@
                 gbuf[2 * s + 1, d, place] = (
                     gbuf[2 * s + 1, d, place].astype(jnp.float32) + ghalf[d, s, inner].astype(jnp.float32)
                 ).astype(jnp.bfloat16)
-            g_full(s, d).start()
+            g_full(s, d, 0).start()
+            g_full(s, d, 1).start()
 
     def master_copy(s):
         return pltpu.make_async_copy(ready.at[s], master.at[:, aligned(s * cw, cw)], m_out.at[s])
 
     def finish(s):
         for d in range(2):
-            g_full(s, d).wait_recv()
+            for h in range(2):
+                g_full(s, d, h).wait_recv()
         scale = 1.0 / (float(rows) * 8.0) ** 0.5
 
         def body(i):
@@ -333,18 +338,23 @@
             total = term if total is None else total + term
         return total
 
+    def sides_of(s):
+        return [aligned(side * quarter + s * cw, cw) for side in range(2)]
+
     def branch_near(s):
         w_ready(s)
-        sides = [aligned(side * quarter + s * cw, cw) for side in range(2)]
 
         def body(t):
             place, cols = near_rows(t // 4), aligned((t % 4) * 256, 256)
-            acc[place, cols] += tile_branch(place, t % 4, sides)
+            acc[place, cols] += tile_branch(place, t % 4, sides_of(s))
 
         each(2 * (feats // 256), body)
 
+    parts = ((0, tok, (0,)), (tok, 2 * tok, (1, 2)), (near, far, (3,)))
+
     def b_sib(part, n):
-        place = ((pl.ds(0, near), pl.ds(near, far))[part], aligned(n * 256, 256))
+        first, count, _ = parts[part]
+        place = (pl.ds(first, count), aligned(n * 256, 256))
         return remote(bsend.at[place], brecv.at[place], b_sib_s.at[part, n], b_sib_r.at[part, n], sib)
 
     def b_out(n, slot):
@@ -355,34 +365,36 @@
             b_out_s.at[n, slot], b_out_r.at[n, slot], at(x + 3, yt, z, c),
         )
 
-    def branch_send(part, first, count, slots):
-        def place(cc):
-            return aligned(cc * count, count, 16)
+    def branch_send(part):
+        first, count, slots = parts[part]
+
+        def value(cc, n):
+            cols = aligned(n * 256, 256)
+            if part == 2:
+                return acc[aligned(cc * far, far, 16), cols]
+            place = aligned(cc * near + first, count, 16)
+            return acc[place, cols] + tile_branch(place, n, sides_of(subs - 1))
 
         def theirs(n):
-            cols = aligned(n * 256, 256)
-            bsend[pl.ds(first, count), cols] = acc[place(oc), cols].astype(jnp.bfloat16)
+            bsend[pl.ds(first, count), aligned(n * 256, 256)] = value(oc, n).astype(jnp.bfloat16)
             b_sib(part, n).start()
-
-        def ours(n):
-            cols = aligned(n * 256, 256)
-            b_sib(part, n).wait_recv()
-            total = acc[place(c), cols] + brecv[pl.ds(first, count), cols].astype(jnp.float32)
-            bout[pl.ds(first, count), cols] = total.astype(jnp.bfloat16)
 
         def send(n):
             for slot in slots:
                 b_out(n, slot).start()
 
+        def ours(n):
+            cols = aligned(n * 256, 256)
+            total = value(c, n)
+            b_sib(part, n).wait_recv()
+            total = total + brecv[pl.ds(first, count), cols].astype(jnp.float32)
+            bout[pl.ds(first, count), cols] = total.astype(jnp.bfloat16)
+            send(n)
+
         @pl.when(x > 0)
         def _():
             each(feats // 256, theirs)
-
-            def both(n):
-                ours(n)
-                send(n)
-
-            each(feats // 256, both)
+            each(feats // 256, ours)
 
         @pl.when(x == 0)
         def _():
@@ -405,29 +417,35 @@
     for t in range(8):
         for one in c_load(t):
             one.start()
-    each(chunks, lambda k: u_local(k).start())
-    each(subs, clip_weights)
+    clip_weights(0)
     pl.semaphore_wait(barrier, greeted)
     for k in range(2):
+        own_mine(k)
         u_sib(k).start()
-        own_mine(k)
+
+    @pl.when(x > 0)
+    def _():
+        for d in range(2):
+            w_own(0, d).start()
+            w_leaf(0, d).start()
 
     pick_batch()
     for part in range(2):
         c_opp(part).start()
+    for k in range(2):
+        own_theirs(k)
+    for p in (2, 3):
+        clip_weights(p)
 
     @pl.when(x > 0)
     def _():
         for u in range(2):
             for d in range(2):
                 w_off(d, u).start()
-        for d in range(2):
-            w_own(0, d).start()
-            w_leaf(0, d).start()
 
     each(chunks - 2, lambda k: u_sib(k + 2).start())
-    for k in range(2):
-        own_theirs(k)
+    each(chunks, lambda k: u_local(k).start())
+    clip_weights(1)
     acc[...] = jnp.zeros_like(acc)
 
     def step(k):
@@ -495,37 +513,42 @@
         def _():
             w_pass_on(3)
 
-        @pl.when((k >= ahead) & (k != 7))
-        def _():
-            grad_chunk(k - ahead)
-
-        @pl.when((x > 0) & (k >= 4) & (k < 8))
-        def _():
-            branch_near(k - 4)
-
-        @pl.when((k == 5) | (k == 7) | (k == 9))
-        def _():
-            combine((k - 5) // 2)
-
         @pl.when(k == 7)
         def _():
             for part in range(2):
                 c_opp(part).wait_send()
-            branch_send(0, 0, near, (0, 1, 2))
-            grad_chunk(k - ahead)
-
-    each(chunks + ahead, step)
+
+            @pl.when(x > 0)
+            def _():
+                w_ready(subs - 1)
+
+            branch_send(0)
+
+        @pl.when((k >= 3) & (k != 7))
+        def _():
+            grad_chunk(k - 3)
+
+        @pl.when((x > 0) & (k >= 4) & (k < 7))
+        def _():
+            branch_near(k - 4)
+
+        @pl.when((k == 5) | (k == 7) | (k == 9))
+        def _():
+            combine((k - 5) // 2)
+
+        @pl.when(k == 7)
+        def _():
+            branch_send(1)
+            grad_chunk(4)
+
+    each(chunks + 3, step)
 
     @pl.when(x > 0)
     def _():
         branch_far()
 
-    branch_send(1, near, far, (3,))
+    branch_send(2)
     combine(3)
-    finish(0)
-    finish(1)
-    finish(2)
-    finish(3)
 
     for part in range(2):
         c_sib(part).wait_send()
@@ -542,7 +565,6 @@
     def drain(s):
         for d in range(2):
             g_half(s, d).wait_send()
-            g_full(s, d).wait_send()
 
         @pl.when(x > 0)
         def _():
@@ -550,12 +572,8 @@
                 w_own(s, d).wait_send()
                 w_leaf(s, d).wait_send()
                 w_fwd(s, d).wait_send()
-            for part in range(2):
+            for part in range(3):
                 b_sib(part, s).wait_send()
-
-        for slot in range(4):
-            b_out(s, slot).wait()
-        master_copy(s).wait()
 
     each(subs, drain)
 
@@ -565,6 +583,18 @@
             for d in range(2):
                 for u in range(2):
                     w_back(plane, d, u).wait_send()
+
+    each(subs, finish)
+
+    def drain_last(s):
+        for d in range(2):
+            for h in range(2):
+                g_full(s, d, h).wait_send()
+        for slot in range(4):
+            b_out(s, slot).wait()
+        master_copy(s).wait()
+
+    each(subs, drain_last)
 
 
 def relay_call(up, saved, weight, noise, levels, plan):
@@ -580,8 +610,8 @@
         (8,), (8,), (8,), (8, 2, 2), (8, 2, 2), (8, 2), (8, 2),
         (8, 2), (2,), (2,), (2,), (2,),
         (4, 2), (4, 2), (4, 2), (4, 2), (4, 2), (4, 2), (4, 2), (3, 2, 2), (3, 2, 2),
-        (4, 2), (4, 2), (4, 2), (4, 2),
-        (2, 4), (2, 4), (4, 4), (4, 4), (4,),
+        (4, 2), (4, 2), (4, 2, 2), (4, 2, 2),
+        (3, 4), (3, 4), (4, 4), (4, 4), (4,),
     ]
     flops = 2 * 2 * brick * feats * span
     anywhere = pl.BlockSpec(memory_space=pl.ANY)
@@ -617,12 +647,12 @@
 
 
 def hand_over(grad, arrived):
-    parts = 8
     pieces = []
     for which, one in enumerate((grad, arrived)):
-        many = parts if one.shape[0] % (parts * 16) == 0 else 1
-        size = one.shape[0] // many
-        pieces += [(which, pl.ds(i * size, size)) for i in range(many)]
+        size = -(-one.shape[0] // (64, 32)[which]) * 16
+        pieces += [
+            (which, pl.ds(begin, min(size, one.shape[0] - begin))) for begin in range(0, one.shape[0], size)
+        ]
 
     def kernel(grad_in, arrived_in, grad_out, arrived_out, grad_held, arrived_held, load_sem, store_sem):
         routes = ((grad_in, grad_held, grad_out), (arrived_in, arrived_held, arrived_out))

time: 165 us -> 162 us (0.982)
  Pallas kernels: 164 us -> 161 us
    pallas_call x1, Pallas kernels: 159 us -> 156 us  [relay_call(): pl.pallas_call(relay_kernel, out_shape=(jax.ShapeDtypeStruct((blk, quarte...]
where the time goes in v4:
time: 162 us
  Pallas kernels  161 us (99%)
    pallas_call x1, Pallas kernels, relay_call(): pl.pallas_call(relay_kernel, out_shape=(jax.ShapeDtypeStruct((blk, quarte...  156 us
    pallas_call x1, Pallas kernels, hand_over(): pl.pallas_call(kernel, out_shape=tuple((jax.ShapeDtypeStruct(one.shape, o...  4.96 us

profile of v4, /device:TPU:6, one launch (start us, length us, event | category | flops | bytes accessed | tf_op | source)
XLA Modules:
  0.0 162.0 jit_solution(17091684741160281196)
XLA Ops:
  0.6 156.4 %relay.1 = (f32[512,2048]{1,0:T(8,128)}, bf16[208,4096]{1,0:T(8,128)(2,1)}) custom-call(bf16[208,8192]{1,0:T(8,128)(2,1)} %bitcast.8, bf16[2,4,2,208,512]{4,3,2,1,0:T(8,128)(2,1)} %bitcast.9, bf16[512,2048]{1,0:T(8,128)(2,1)} %bitcast.10, bf16[512,2048]{1,0:T(8,128)(2,1)} %bitcast.11, s32[4,16]{1,0:T(4,128)} %bitcast.13, s32[4]{0:T(128)} %plan.1), custom_call_target="tpu_custom_call" | custom-call | flops 27917287424 | bytes 33554432 | tf_op jit(solution)/shard_map/relay/pallas_call | solution.py:619
  157.1 5.0 %hand_over.1 = (f32[512,2048]{1,0:T(8,128)}, bf16[208,4096]{1,0:T(8,128)(2,1)}) custom-call(f32[512,2048]{1,0:T(8,128)} %get-tuple-element.6.grad_in, bf16[208,4096]{1,0:T(8,128)(2,1)} %get-tuple-element.7.arrived_in), custom_call_target="tpu_custom_call" | custom-call | tf_op jit(solution)/shard_map/hand_over/pallas_call | solution.py:673

commit v5 on v4

--- a/solution.py
+++ b/solution.py
@@ -56,6 +56,10 @@
     zp = (zh + zl) % 2
     zside = (zp, 1 - zp)
 
+    for place in (pl.ds(0, cw),):
+        pltpu.make_async_copy(weight_in.at[:, place], weight.at[:, place], w_loc.at[0, 0]).start()
+        pltpu.make_async_copy(noise_in.at[:, place], noise.at[:, place], w_loc.at[0, 1]).start()
+
     barrier = pltpu.get_barrier_semaphore()
     greet = [sib, opp, *ynb, *znb] + [at(x + 1, y + j, z, c) for j in range(4)]
     for one in greet:
@@ -280,11 +284,8 @@
             gbuf.at[2 * s, 1, pl.ds(d * half, half)], ghalf.at[d, s], g_half_s.at[s, d], g_half_r.at[s, d], znb[d]
         )
 
-    def g_full(s, d, h):
-        place = pl.ds(h * half, half)
-        return remote(
-            gbuf.at[2 * s + 1, d, place], gfull.at[d, s, place], g_full_s.at[s, d, h], g_full_r.at[s, d, h], znb[d]
-        )
+    def g_full(s, d):
+        return remote(gbuf.at[2 * s + 1, d], gfull.at[d, s], g_full_s.at[s, d], g_full_r.at[s, d], znb[d])
 
     def combine(s):
         for d in range(2):
@@ -295,16 +296,14 @@
                 gbuf[2 * s + 1, d, place] = (
                     gbuf[2 * s + 1, d, place].astype(jnp.float32) + ghalf[d, s, inner].astype(jnp.float32)
                 ).astype(jnp.bfloat16)
-            g_full(s, d, 0).start()
-            g_full(s, d, 1).start()
+            g_full(s, d).start()
 
     def master_copy(s):
         return pltpu.make_async_copy(ready.at[s], master.at[:, aligned(s * cw, cw)], m_out.at[s])
 
     def finish(s):
         for d in range(2):
-            for h in range(2):
-                g_full(s, d, h).wait_recv()
+            g_full(s, d).wait_recv()
         scale = 1.0 / (float(rows) * 8.0) ** 0.5
 
         def body(i):
@@ -411,13 +410,13 @@
 
         each(feats // 256, body)
 
-    for p in range(subs):
-        for one in w_load(p):
-            one.start()
     for t in range(8):
         for one in c_load(t):
             one.start()
     clip_weights(0)
+    for p in range(1, subs):
+        for one in w_load(p):
+            one.start()
     pl.semaphore_wait(barrier, greeted)
     for k in range(2):
         own_mine(k)
@@ -584,17 +583,20 @@
                 for u in range(2):
                     w_back(plane, d, u).wait_send()
 
-    each(subs, finish)
+    each(subs - 1, finish)
 
     def drain_last(s):
-        for d in range(2):
-            for h in range(2):
-                g_full(s, d, h).wait_send()
         for slot in range(4):
             b_out(s, slot).wait()
+
+    each(subs, drain_last)
+    for s in range(subs - 1):
         master_copy(s).wait()
-
-    each(subs, drain_last)
+    finish(subs - 1)
+    for s in range(subs):
+        for d in range(2):
+            g_full(s, d).wait_send()
+    master_copy(subs - 1).wait()
 
 
 def relay_call(up, saved, weight, noise, levels, plan):
@@ -610,7 +612,7 @@
         (8,), (8,), (8,), (8, 2, 2), (8, 2, 2), (8, 2), (8, 2),
         (8, 2), (2,), (2,), (2,), (2,),
         (4, 2), (4, 2), (4, 2), (4, 2), (4, 2), (4, 2), (4, 2), (3, 2, 2), (3, 2, 2),
-        (4, 2), (4, 2), (4, 2, 2), (4, 2, 2),
+        (4, 2), (4, 2), (4, 2), (4, 2),
         (3, 4), (3, 4), (4, 4), (4, 4), (4,),
     ]
     flops = 2 * 2 * brick * feats * span
@@ -649,7 +651,7 @@
 def hand_over(grad, arrived):
     pieces = []
     for which, one in enumerate((grad, arrived)):
-        size = -(-one.shape[0] // (64, 32)[which]) * 16
+        size = -(-one.shape[0] // (32, 32)[which]) * 16
         pieces += [
             (which, pl.ds(begin, min(size, one.shape[0] - begin))) for begin in range(0, one.shape[0], size)
         ]

time: 162 us -> 160 us (0.988)
  no operation moved by 1% of the time
where the time goes in v5:
time: 160 us
  Pallas kernels  160 us (100%)
    pallas_call x1, Pallas kernels, relay_call(): pl.pallas_call(relay_kernel, out_shape=(jax.ShapeDtypeStruct((blk, quarte...  155 us
    pallas_call x1, Pallas kernels, hand_over(): pl.pallas_call(kernel, out_shape=tuple((jax.ShapeDtypeStruct(one.shape, o...  4.2 us

profile of v5, /device:TPU:6, one launch (start us, length us, event | category | flops | bytes accessed | tf_op | source)
XLA Modules:
  0.0 160.3 jit_solution(6646743751330062715)
XLA Ops:
  0.6 155.5 %relay.1 = (f32[512,2048]{1,0:T(8,128)}, bf16[208,4096]{1,0:T(8,128)(2,1)}) custom-call(bf16[208,8192]{1,0:T(8,128)(2,1)} %bitcast.8, bf16[2,4,2,208,512]{4,3,2,1,0:T(8,128)(2,1)} %bitcast.9, bf16[512,2048]{1,0:T(8,128)(2,1)} %bitcast.10, bf16[512,2048]{1,0:T(8,128)(2,1)} %bitcast.11, s32[4,16]{1,0:T(4,128)} %bitcast.13, s32[4]{0:T(128)} %plan.1), custom_call_target="tpu_custom_call" | custom-call | flops 27917287424 | bytes 33554432 | tf_op jit(solution)/shard_map/relay/pallas_call | solution.py:621
  156.1 4.2 %hand_over.1 = (f32[512,2048]{1,0:T(8,128)}, bf16[208,4096]{1,0:T(8,128)(2,1)}) custom-call(f32[512,2048]{1,0:T(8,128)} %get-tuple-element.6.grad_in, bf16[208,4096]{1,0:T(8,128)(2,1)} %get-tuple-element.7.arrived_in), custom_call_target="tpu_custom_call" | custom-call | tf_op jit(solution)/shard_map/hand_over/pallas_call | solution.py:675

commit v6 on v5

--- a/solution.py
+++ b/solution.py
@@ -438,9 +438,8 @@
 
     @pl.when(x > 0)
     def _():
-        for u in range(2):
-            for d in range(2):
-                w_off(d, u).start()
+        for d in range(2):
+            w_off(d, 0).start()
 
     each(chunks - 2, lambda k: u_sib(k + 2).start())
     each(chunks, lambda k: u_local(k).start())
@@ -477,6 +476,11 @@
                 for d in range(2):
                     w_off_wait(plane, d, u).wait_recv()
                     w_back(plane, d, u).start()
+
+        @pl.when((x > 0) & (k == 0))
+        def _():
+            for d in range(2):
+                w_off(d, 1).start()
 
         @pl.when((x > 0) & (k == 1))
         def _():

time: 160 us -> 160 us (level)
  no operation moved by 1% of the time
where the time goes in v6:
time: 160 us
  Pallas kernels  160 us (100%)
    pallas_call x1, Pallas kernels, relay_call(): pl.pallas_call(relay_kernel, out_shape=(jax.ShapeDtypeStruct((blk, quarte...  155 us
    pallas_call x1, Pallas kernels, hand_over(): pl.pallas_call(kernel, out_shape=tuple((jax.ShapeDtypeStruct(one.shape, o...  4.2 us

profile of v6, /device:TPU:6, one launch (start us, length us, event | category | flops | bytes accessed | tf_op | source)
XLA Modules:
  0.0 160.3 jit_solution(5005427697719671661)
XLA Ops:
  0.6 155.5 %relay.1 = (f32[512,2048]{1,0:T(8,128)}, bf16[208,4096]{1,0:T(8,128)(2,1)}) custom-call(bf16[208,8192]{1,0:T(8,128)(2,1)} %bitcast.8, bf16[2,4,2,208,512]{4,3,2,1,0:T(8,128)(2,1)} %bitcast.9, bf16[512,2048]{1,0:T(8,128)(2,1)} %bitcast.10, bf16[512,2048]{1,0:T(8,128)(2,1)} %bitcast.11, s32[4,16]{1,0:T(4,128)} %bitcast.13, s32[4]{0:T(128)} %plan.1), custom_call_target="tpu_custom_call" | custom-call | flops 27917287424 | bytes 33554432 | tf_op jit(solution)/shard_map/relay/pallas_call | solution.py:625
  156.1 4.2 %hand_over.1 = (f32[512,2048]{1,0:T(8,128)}, bf16[208,4096]{1,0:T(8,128)(2,1)}) custom-call(f32[512,2048]{1,0:T(8,128)} %get-tuple-element.6.grad_in, bf16[208,4096]{1,0:T(8,128)(2,1)} %get-tuple-element.7.arrived_in), custom_call_target="tpu_custom_call" | custom-call | tf_op jit(solution)/shard_map/hand_over/pallas_call | solution.py:679

commit v7 on v5

--- a/solution.py
+++ b/solution.py
@@ -298,8 +298,9 @@
                 ).astype(jnp.bfloat16)
             g_full(s, d).start()
 
-    def master_copy(s):
-        return pltpu.make_async_copy(ready.at[s], master.at[:, aligned(s * cw, cw)], m_out.at[s])
+    def master_copy(s, i):
+        line = aligned(i * TILE, TILE)
+        return pltpu.make_async_copy(ready.at[s, line], master.at[line, aligned(s * cw, cw)], m_out.at[s, i])
 
     def finish(s):
         for d in range(2):
@@ -316,9 +317,9 @@
                 total = gbuf[2 * s, 0, line, inner].astype(jnp.float32) + gfull[0, s, line, inner].astype(jnp.float32)
                 total = total + gfull[1, s, line, inner].astype(jnp.float32)
                 ready[s, line, inner] = jnp.where(jnp.abs(noisy) <= bound, total * scale, 0.0)
+            master_copy(s, i).start()
 
         each(blk // TILE, body)
-        master_copy(s).start()
 
     def w_ready(p):
         for d in range(2):
@@ -591,12 +592,14 @@
 
     each(subs, drain_last)
     for s in range(subs - 1):
-        master_copy(s).wait()
+        for i in range(blk // TILE):
+            master_copy(s, i).wait()
     finish(subs - 1)
     for s in range(subs):
         for d in range(2):
             g_full(s, d).wait_send()
-    master_copy(subs - 1).wait()
+    for i in range(blk // TILE):
+        master_copy(subs - 1, i).wait()
 
 
 def relay_call(up, saved, weight, noise, levels, plan):
@@ -613,7 +616,7 @@
         (8, 2), (2,), (2,), (2,), (2,),
         (4, 2), (4, 2), (4, 2), (4, 2), (4, 2), (4, 2), (4, 2), (3, 2, 2), (3, 2, 2),
         (4, 2), (4, 2), (4, 2), (4, 2),
-        (3, 4), (3, 4), (4, 4), (4, 4), (4,),
+        (3, 4), (3, 4), (4, 4), (4, 4), (4, 4),
     ]
     flops = 2 * 2 * brick * feats * span
     anywhere = pl.BlockSpec(memory_space=pl.ANY)

time: 160 us -> 160 us (level)
  no operation moved by 1% of the time
where the time goes in v7:
time: 160 us
  Pallas kernels  159 us (99%)
    pallas_call x1, Pallas kernels, relay_call(): pl.pallas_call(relay_kernel, out_shape=(jax.ShapeDtypeStruct((blk, quarte...  155 us
    pallas_call x1, Pallas kernels, hand_over(): pl.pallas_call(kernel, out_shape=tuple((jax.ShapeDtypeStruct(one.shape, o...  4.2 us

profile of v7, /device:TPU:6, one launch (start us, length us, event | category | flops | bytes accessed | tf_op | source)
XLA Modules:
  0.0 160.1 jit_solution(5270504398410961039)
XLA Ops:
  0.6 155.3 %relay.1 = (f32[512,2048]{1,0:T(8,128)}, bf16[208,4096]{1,0:T(8,128)(2,1)}) custom-call(bf16[208,8192]{1,0:T(8,128)(2,1)} %bitcast.8, bf16[2,4,2,208,512]{4,3,2,1,0:T(8,128)(2,1)} %bitcast.9, bf16[512,2048]{1,0:T(8,128)(2,1)} %bitcast.10, bf16[512,2048]{1,0:T(8,128)(2,1)} %bitcast.11, s32[4,16]{1,0:T(4,128)} %bitcast.13, s32[4]{0:T(128)} %plan.1), custom_call_target="tpu_custom_call" | custom-call | flops 27917287424 | bytes 33554432 | tf_op jit(solution)/shard_map/relay/pallas_call | solution.py:624
  155.9 4.2 %hand_over.1 = (f32[512,2048]{1,0:T(8,128)}, bf16[208,4096]{1,0:T(8,128)(2,1)}) custom-call(f32[512,2048]{1,0:T(8,128)} %get-tuple-element.6.grad_in, bf16[208,4096]{1,0:T(8,128)(2,1)} %get-tuple-element.7.arrived_in), custom_call_target="tpu_custom_call" | custom-call | tf_op jit(solution)/shard_map/hand_over/pallas_call | solution.py:678
